TPU v7x, 256 devices: a whole 4x4x8 slice. The times are simulated.
256 devices in a mesh: dp: 16 (over z, core), owner: 16 (over x, y).
Axes of the slice: x: 4, y: 4, z: 8, core: 2. Of those that a mesh axis runs over, the one named last changes fastest.
Arguments:
- partials: bfloat16 [16, 128, 512, 512], P('dp', None, 'owner'), may hold values from -0.25 to 0.25
- l_factor: float32 [256, 512, 512], P(('dp', 'owner')), as said below
- r_factor: float32 [256, 512, 512], P(('dp', 'owner')), as said below
- l_root: bfloat16 [256, 512, 512], P(('dp', 'owner')), as said below
- r_root: bfloat16 [256, 512, 512], P(('dp', 'owner')), as said below
- owner_table: int32 [16, 8], replicated, may hold values from 0 to 15, as said below
Outputs:
- preconditioned: bfloat16 [128, 512, 512], P('dp', 'owner')
- new_l_factor: float32 [256, 512, 512], P(('dp', 'owner'))
- new_r_factor: float32 [256, 512, 512], P(('dp', 'owner'))
- new_l_root: bfloat16 [256, 512, 512], P(('dp', 'owner'))
- new_r_root: bfloat16 [256, 512, 512], P(('dp', 'owner'))
Inputs may be any that keep to these rules, and one draw needn't show every extreme that they name: `owner_table`: each row names 8 different owner indices. `l_factor`: symmetric positive definite. `r_factor`: symmetric positive definite. `l_root`: Symmetric. `r_root`: Symmetric.
All inputs are finite; a program needn't handle non-finite values.
Results may differ from a plain program's by a relative error of at most 0.04.
Values may be sent and summed in bfloat16 or wider, within the bound.
No kernel may reach another device: no remote copies, remote signals or barrier semaphores. Data moves between devices by JAX's collectives and lax.ppermute only.
A program may use at most 128 MiB of HBM per device.

v0:
```python
import jax
import jax.numpy as jnp
from jax import lax
from jax.sharding import PartitionSpec as P

NEWTON = 2


BETA = 0.9


def matmul_high(left, right):
    return jnp.dot(left, right, precision=lax.Precision.HIGHEST, preferred_element_type=jnp.float32)


def inverse_root(factor, root):
    identity = jnp.eye(factor.shape[0], dtype=jnp.float32)
    current = root.astype(jnp.float32)
    square = matmul_high(current, current)
    fourth = matmul_high(square, square)
    product = matmul_high(fourth, factor)
    for newton_turn in range(NEWTON):
        step_matrix = (5.0 * identity - product) * 0.25
        current = matmul_high(current, step_matrix)
        if newton_turn + 1 < NEWTON:
            step_square = matmul_high(step_matrix, step_matrix)
            step_fourth = matmul_high(step_square, step_square)
            product = matmul_high(step_fourth, product)
    return current.astype(jnp.bfloat16)


def update_block(gradient, l_old, r_old, l_inv, r_inv):
    left_gram = jnp.dot(gradient, gradient.T, preferred_element_type=jnp.float32)
    right_gram = jnp.dot(gradient.T, gradient, preferred_element_type=jnp.float32)
    l_new = BETA * l_old + (1.0 - BETA) * left_gram
    r_new = BETA * r_old + (1.0 - BETA) * right_gram
    left_applied = jnp.dot(l_inv, gradient, preferred_element_type=jnp.float32).astype(jnp.bfloat16)
    precond = jnp.dot(left_applied, r_inv, preferred_element_type=jnp.float32).astype(jnp.bfloat16)
    return (l_new, r_new, inverse_root(l_new, l_inv), inverse_root(r_new, r_inv), precond)


def body(partials, l_factor, r_factor, l_root, r_root, owner_table):
    owners = lax.axis_size("owner")
    group_index = lax.axis_index("dp")
    owner_index = lax.axis_index("owner")
    my_row = lax.dynamic_index_in_dim(owner_table, group_index, 0, keepdims=False)
    local_rows = partials[0]
    slice_rows = local_rows.shape[1]
    row_width = local_rows.shape[2]
    row_blocks = my_row.shape[0]
    owner_ids = jnp.arange(owners, dtype=jnp.int32)
    summed = lax.psum_scatter(
        local_rows.astype(jnp.float32).astype(jnp.bfloat16), "dp", scatter_dimension=0, tiled=True
    )
    select = (owner_ids[:, None] == my_row[None, :]).astype(jnp.bfloat16)
    outgoing = jnp.dot(
        select,
        summed.reshape(row_blocks, slice_rows * row_width),
        preferred_element_type=jnp.float32,
    )
    outgoing = outgoing.astype(jnp.bfloat16).reshape(owners, slice_rows, row_width)
    arrived = lax.all_to_all(outgoing, "owner", split_axis=0, concat_axis=0, tiled=True)
    gradient = arrived.reshape(owners * slice_rows, row_width)
    is_owner = jnp.any(my_row == owner_index)
    l_new, r_new, l_next, r_next, precond = update_block(
        gradient, l_factor[0], r_factor[0], l_root[0], r_root[0]
    )
    l_out = jnp.where(is_owner, l_new, l_factor[0])[None]
    r_out = jnp.where(is_owner, r_new, r_factor[0])[None]
    l_root_out = jnp.where(is_owner, l_next, l_root[0])[None]
    r_root_out = jnp.where(is_owner, r_next, r_root[0])[None]
    precond = jnp.where(is_owner, precond, jnp.zeros_like(precond))
    returned = lax.all_to_all(
        precond.reshape(owners, slice_rows, row_width),
        "owner",
        split_axis=0,
        concat_axis=0,
        tiled=True,
    )
    select_back = (my_row[:, None] == owner_ids[None, :]).astype(jnp.bfloat16)
    my_blocks = jnp.dot(
        select_back,
        returned.reshape(owners, slice_rows * row_width),
        preferred_element_type=jnp.float32,
    )
    my_blocks = my_blocks.astype(jnp.bfloat16).reshape(row_blocks, slice_rows, row_width)
    return (my_blocks, l_out, r_out, l_root_out, r_root_out)


def solution(mesh):
    placed = (
        P("dp", None, "owner", None),
        P(("dp", "owner"), None, None),
        P(("dp", "owner"), None, None),
        P(("dp", "owner"), None, None),
        P(("dp", "owner"), None, None),
        P(),
    )
    return jax.shard_map(
        body,
        mesh=mesh,
        in_specs=placed,
        out_specs=(
            P("dp", "owner", None),
            P(("dp", "owner"), None, None),
            P(("dp", "owner"), None, None),
            P(("dp", "owner"), None, None),
            P(("dp", "owner"), None, None),
        ),
        check_vma=False,
    )
```

profile of v0, /device:TPU:4, one launch (start us, length us, event | category | flops | bytes accessed | tf_op | source)
XLA Modules:
  0.0 151.5 jit_solution(5719975285640836662)
XLA Ops:
  7.2 0.7 reduce-scatter.2.cloned.1.call-update
  8.2 0.4 fusion.27
  8.7 2.8 %fusion.57 = f32[512,512]{1,0:T(8,128)} fusion(f32[512,512]{1,0:T(8,128)S(1)} %fusion.27), kind=kOutput, calls=%fused_computation.73 | convolution fusion | flops 1610612736 | bytes 2097152 | tf_op jit(solution)/shard_map/dot_general | solution.py:13
  11.5 64.7 %reduce-scatter.2.cloned.1.call-done = bf16[8,32,512]{2,1,0:T(8,128)(2,1)} async-done(((bf16[128,32,512]{2,1,0:T(8,128)(2,1)}), bf16[8,32,512]{2,1,0:T(8,128)(2,1)}) %reduce-scatter.2.cloned.1.call-update) | async-done | bytes 262160 | tf_op jit(solution)/shard_map/reduce_scatter | solution.py:52
  76.2 1.1 copy.12
  77.3 0.3 convolution_convert_fusion
  77.6 1.0 copy.13
  78.5 7.3 %all-to-all-start = ((bf16[16,32,512]{2,1,0:T(8,128)(2,1)}), bf16[16,32,512]{2,1,0:T(8,128)(2,1)S(1)}, u32[]{:S(2)}, u32[]{:S(2)}) async-start(bf16[16,32,512]{2,1,0:T(8,128)(2,1)} %bitcast.16), calls=%async_computation.1 | async-start | bytes 1048576 | tf_op jit(solution)/shard_map/all_to_all | solution.py:62
  85.8 0.4 fusion.23
  86.3 0.6 compare_reduce_fusion
  86.9 2.8 %fusion.60 = f32[512,512]{1,0:T(8,128)} fusion(f32[512,512]{1,0:T(8,128)S(1)} %fusion.23), kind=kOutput, calls=%fused_computation.76 | convolution fusion | flops 1610612736 | bytes 2097152 | tf_op jit(solution)/shard_map/dot_general | solution.py:13
  89.7 3.8 %all-to-all-done = bf16[16,32,512]{2,1,0:T(8,128)(2,1)S(1)} async-done(((bf16[16,32,512]{2,1,0:T(8,128)(2,1)}), bf16[16,32,512]{2,1,0:T(8,128)(2,1)S(1)}, u32[]{:S(2)}, u32[]{:S(2)}) %all-to-all-start) | async-done | bytes 524320 | tf_op jit(solution)/shard_map/all_to_all | solution.py:62
  93.6 1.9 %fusion.1 = f32[512,512]{1,0:T(8,128)S(1)} fusion(bf16[512,512]{1,0:T(8,128)(2,1)S(1)} %bitcast.82, f32[1,512,512]{2,1,0:T(8,128)} %param.7), kind=kOutput, calls=%fused_computation.9 | convolution fusion | flops 269221888 | bytes 2621440 | tf_op jit(solution)/shard_map/dot_general | solution.py:33
  95.5 3.2 %fusion.58 = f32[512,512]{1,0:T(8,128)S(1)} fusion(f32[512,512]{1,0:T(8,128)} %fusion.57, f32[512,512]{1,0:T(8,128)S(1)} %fusion.1), kind=kOutput, calls=%fused_computation.74 | convolution fusion | flops 1610612736 | bytes 3145728 | tf_op jit(solution)/shard_map/dot_general | solution.py:13
  98.6 2.9 %fusion.18 = f32[512,512]{1,0:T(8,128)} fusion(f32[512,512]{1,0:T(8,128)S(1)} %fusion.58), kind=kOutput, calls=%fused_computation.33 | convolution fusion | flops 1611661312 | bytes 2097152 | tf_op jit(solution)/shard_map/dot_general | solution.py:13
  101.5 2.9 %fusion.20 = f32[512,512]{1,0:T(8,128)} fusion(f32[512,512]{1,0:T(8,128)S(1)} %fusion.58, bf16[1,512,512]{2,1,0:T(8,128)(2,1)S(1)} %copy-done.3), kind=kOutput, calls=%fused_computation.34 | convolution fusion | flops 1611661312 | bytes 2621440 | tf_op jit(solution)/shard_map/dot_general | solution.py:13
  104.4 0.5 fusion.4
  104.9 1.0 copy-done.9
  105.9 1.9 %fusion.61 = f32[512,512]{1,0:T(8,128)S(1)} fusion(f32[512,512]{1,0:T(8,128)S(1)} %copy-done.11, f32[512,512]{1,0:T(8,128)S(1)} %fusion.4), kind=kOutput, calls=%fused_computation.77 | convolution fusion | flops 1610612736 | bytes 3145728 | tf_op jit(solution)/shard_map/dot_general | solution.py:13
  107.7 2.9 %fusion.14 = f32[512,512]{1,0:T(8,128)} fusion(f32[512,512]{1,0:T(8,128)S(1)} %fusion.61), kind=kOutput, calls=%fused_computation.31 | convolution fusion | flops 1611661312 | bytes 2097152 | tf_op jit(solution)/shard_map/dot_general | solution.py:13
  110.6 3.1 %fusion.16 = f32[512,512]{1,0:T(8,128)} fusion(f32[512,512]{1,0:T(8,128)S(1)} %fusion.61, bf16[1,512,512]{2,1,0:T(8,128)(2,1)S(1)} %copy-done.6), kind=kOutput, calls=%fused_computation.32 | convolution fusion | flops 1611661312 | bytes 2621440 | tf_op jit(solution)/shard_map/dot_general | solution.py:13
  113.7 3.7 %fusion.5 = bf16[512,512]{1,0:T(8,128)(2,1)} fusion(bf16[512,512]{1,0:T(8,128)(2,1)} %bitcast.83, bf16[1,512,512]{2,1,0:T(8,128)(2,1)} %param.10, bf16[1,512,512]{2,1,0:T(8,128)(2,1)} %param.9, pred[]{:T(512)} %compare_reduce_fusion), kind=kOutput, calls=%fused_computation.17 | convolution fusion | flops 537657344 | bytes 2097153 | tf_op jit(solution)/shard_map/dot_general | solution.py:38
  117.4 6.5 %all-to-all-start.1 = ((bf16[16,32,512]{2,1,0:T(8,128)(2,1)}), bf16[16,32,512]{2,1,0:T(8,128)(2,1)}, u32[]{:S(2)}, u32[]{:S(2)}) async-start(bf16[16,32,512]{2,1,0:T(8,128)(2,1)} %bitcast.89), calls=%async_computation.2 | async-start | bytes 1048576 | tf_op jit(solution)/shard_map/all_to_all | solution.py:73
  123.9 3.5 %fusion.59 = f32[512,512]{1,0:T(8,128)S(1)} fusion(f32[512,512]{1,0:T(8,128)} %fusion.18), kind=kOutput, calls=%fused_computation.75 | convolution fusion | flops 1610612736 | bytes 2097152 | tf_op jit(solution)/shard_map/dot_general | solution.py:13
  127.4 1.9 %fusion.2 = f32[512,512]{1,0:T(8,128)S(1)} fusion(f32[512,512]{1,0:T(8,128)S(1)} %fusion.59, f32[512,512]{1,0:T(8,128)S(1)} %fusion.58), kind=kOutput, calls=%fused_computation.10 | convolution fusion | flops 1611661312 | bytes 3145728 | tf_op jit(solution)/shard_map/dot_general | solution.py:13
  129.3 1.8 %fusion.62 = f32[512,512]{1,0:T(8,128)S(1)} fusion(f32[512,512]{1,0:T(8,128)S(1)} %copy-done.1), kind=kOutput, calls=%fused_computation.78 | convolution fusion | flops 1610612736 | bytes 2097152 | tf_op jit(solution)/shard_map/dot_general | solution.py:13
  131.2 1.9 %fusion.3 = f32[512,512]{1,0:T(8,128)S(1)} fusion(f32[512,512]{1,0:T(8,128)S(1)} %fusion.62, f32[512,512]{1,0:T(8,128)S(1)} %fusion.61), kind=kOutput, calls=%fused_computation.11 | convolution fusion | flops 1611661312 | bytes 3145728 | tf_op jit(solution)/shard_map/dot_general | solution.py:13
  133.0 3.4 %fusion.7 = bf16[1,512,512]{2,1,0:T(8,128)(2,1)} fusion(f32[512,512]{1,0:T(8,128)S(1)} %copy-done.12, f32[512,512]{1,0:T(8,128)S(1)} %fusion.2, bf16[1,512,512]{2,1,0:T(8,128)(2,1)S(1)} %copy-done.4, pred[]{:T(512)} %compare_reduce_fusion), kind=kOutput, calls=%fused_computation.19 | convolution fusion | flops 1611137024 | bytes 3145729 | tf_op jit(solution)/shard_map/dot_general | solution.py:13
  136.4 3.4 %fusion.9 = bf16[1,512,512]{2,1,0:T(8,128)(2,1)} fusion(f32[512,512]{1,0:T(8,128)S(1)} %copy-done.13, f32[512,512]{1,0:T(8,128)S(1)} %fusion.3, bf16[1,512,512]{2,1,0:T(8,128)(2,1)S(1)} %copy-done.7, pred[]{:T(512)} %compare_reduce_fusion), kind=kOutput, calls=%fused_computation.21 | convolution fusion | flops 1611137024 | bytes 3145729 | tf_op jit(solution)/shard_map/dot_general | solution.py:13
  139.8 2.4 %fusion.12 = (f32[1,512,512]{2,1,0:T(8,128)}, f32[1,512,512]{2,1,0:T(8,128)}) fusion(f32[512,512]{1,0:T(8,128)S(1)} %copy-done.10, f32[1,512,512]{2,1,0:T(8,128)S(1)} %copy-done.15, pred[]{:T(512)} %compare_reduce_fusion, f32[512,512]{1,0:T(8,128)S(1)} %fusion.1, f32[1,512,512]{2,1,0:T(8,128)S(1)} %copy-done.8), kind=kLoop, calls=%fused_computation.26 | loop fusion | flops 524288 | bytes 6291457 | tf_op jit(solution)/shard_map/broadcast_in_dim | solution.py:69
  142.2 1.3 copy.14
  143.8 0.8 copy.11
  (35 shorter events, 0.7 us)
Async XLA Ops:
  7.2 0.8 copy-start
  7.2 1.0 copy-start.3
  7.2 69.0 %reduce-scatter.2.cloned.1.call-start = ((), (), s32[]{:S(2)}) async-start(), calls=%async_computation.3 | async-start | bytes 4456448 | tf_op jit(solution)/shard_map/reduce_scatter | solution.py:52
  7.9 77.9 %copy-start.5 = (bf16[1,512,512]{2,1,0:T(8,128)(2,1)S(1)}, bf16[1,512,512]{2,1,0:T(8,128)(2,1)}, u32[]{:S(2)}) copy-start(bf16[1,512,512]{2,1,0:T(8,128)(2,1)} %param.10) | copy-start | bytes 1572868
  78.5 15.0 %all-to-all-start = ((bf16[16,32,512]{2,1,0:T(8,128)(2,1)}), bf16[16,32,512]{2,1,0:T(8,128)(2,1)S(1)}, u32[]{:S(2)}, u32[]{:S(2)}) async-start(bf16[16,32,512]{2,1,0:T(8,128)(2,1)} %bitcast.16), calls=%async_computation.1 | async-start | bytes 1048576 | tf_op jit(solution)/shard_map/all_to_all | solution.py:62
  93.6 10.8 %copy-start.2 = (bf16[16,32,512]{2,1,0:T(8,128)(2,1)}, bf16[16,32,512]{2,1,0:T(8,128)(2,1)S(1)}, u32[]{:S(2)}) copy-start(bf16[16,32,512]{2,1,0:T(8,128)(2,1)S(1)} %all-to-all-done) | copy-start | bytes 1572868
  95.5 8.9 %copy-start.14 = (f32[1,512,512]{2,1,0:T(8,128)S(1)}, f32[1,512,512]{2,1,0:T(8,128)}, u32[]{:S(2)}) copy-start(f32[1,512,512]{2,1,0:T(8,128)} %param.8) | copy-start | bytes 3145732
  104.4 1.5 copy-start.11
  104.9 1.0 copy-start.9
  105.9 4.8 %copy-start.6 = (bf16[1,512,512]{2,1,0:T(8,128)(2,1)S(1)}, bf16[1,512,512]{2,1,0:T(8,128)(2,1)}, u32[]{:S(2)}) copy-start(bf16[1,512,512]{2,1,0:T(8,128)(2,1)} %param.10) | copy-start | bytes 1572868
  117.4 24.8 %all-to-all-start.1 = ((bf16[16,32,512]{2,1,0:T(8,128)(2,1)}), bf16[16,32,512]{2,1,0:T(8,128)(2,1)}, u32[]{:S(2)}, u32[]{:S(2)}) async-start(bf16[16,32,512]{2,1,0:T(8,128)(2,1)} %bitcast.89), calls=%async_computation.2 | async-start | bytes 1048576 | tf_op jit(solution)/shard_map/all_to_all | solution.py:73
  123.9 5.4 %copy-start.1 = (f32[512,512]{1,0:T(8,128)S(1)}, f32[512,512]{1,0:T(8,128)}, u32[]{:S(2)}) copy-start(f32[512,512]{1,0:T(8,128)} %fusion.14) | copy-start | bytes 3145732
  127.3 5.7 %copy-start.4 = (bf16[1,512,512]{2,1,0:T(8,128)(2,1)S(1)}, bf16[1,512,512]{2,1,0:T(8,128)(2,1)}, u32[]{:S(2)}) copy-start(bf16[1,512,512]{2,1,0:T(8,128)(2,1)} %param.9) | copy-start | bytes 1572868
  127.4 5.7 %copy-start.12 = (f32[512,512]{1,0:T(8,128)S(1)}, f32[512,512]{1,0:T(8,128)}, u32[]{:S(2)}) copy-start(f32[512,512]{1,0:T(8,128)} %fusion.20) | copy-start | bytes 3145732
  129.2 7.2 %copy-start.7 = (bf16[1,512,512]{2,1,0:T(8,128)(2,1)S(1)}, bf16[1,512,512]{2,1,0:T(8,128)(2,1)}, u32[]{:S(2)}) copy-start(bf16[1,512,512]{2,1,0:T(8,128)(2,1)} %param.10) | copy-start | bytes 1572868
  129.3 7.1 %copy-start.13 = (f32[512,512]{1,0:T(8,128)S(1)}, f32[512,512]{1,0:T(8,128)}, u32[]{:S(2)}) copy-start(f32[512,512]{1,0:T(8,128)} %fusion.16) | copy-start | bytes 3145732
  131.1 8.6 %copy-start.8 = (f32[1,512,512]{2,1,0:T(8,128)S(1)}, f32[1,512,512]{2,1,0:T(8,128)}, u32[]{:S(2)}) copy-start(f32[1,512,512]{2,1,0:T(8,128)} %param.7) | copy-start | bytes 3145732
  131.1 8.6 %copy-start.10 = (f32[512,512]{1,0:T(8,128)S(1)}, f32[512,512]{1,0:T(8,128)}, u32[]{:S(2)}) copy-start(f32[512,512]{1,0:T(8,128)} %copy-done.9) | copy-start | bytes 3145732
  131.1 8.6 %copy-start.15 = (f32[1,512,512]{2,1,0:T(8,128)S(1)}, f32[1,512,512]{2,1,0:T(8,128)}, u32[]{:S(2)}) copy-start(f32[1,512,512]{2,1,0:T(8,128)} %param.8) | copy-start | bytes 3145732
Sparse Core Ops, SparseCore 0:
  10.6 65.5 reduce-scatter.1
where the time goes:
time: 152 us; the launch traced here: 151 us
  waiting for transfers between devices  69.2 us (46%)
  matrix products  45.6 us (30%)
  between operations  14.3 us (9%)
  starting transfers between devices  13.8 us (9%)
  local copies, waits for them, and re-layouts  5.5 us (4%)
  other arithmetic  3.07 us (2%)
    reduce_scatter x1, waiting for transfers between devices, body(): lax.psum_scatter(local_rows.astype(jnp.float32).astype(jnp.bfloat16), 'dp...  64.7 us
    dot_general x16, matrix products, matmul_high(): jnp.dot(left, right, precision=lax.Precision.HIGHEST, preferred_element_t...  39 us
    all_to_all x1, starting transfers between devices, body(): lax.all_to_all(outgoing, 'owner', split_axis=0, concat_axis=0, tiled=True)  7.29 us
    all_to_all x1, starting transfers between devices, body(): lax.all_to_all(precond.reshape(owners, slice_rows, row_width), 'owner', s...  6.47 us
    unnamed x36, local copies, waits for them, and re-layouts  5.31 us
    all_to_all x1, waiting for transfers between devices, body(): lax.all_to_all(outgoing, 'owner', split_axis=0, concat_axis=0, tiled=True)  3.82 us
    dot_general x1, matrix products, update_block(): jnp.dot(left_applied, r_inv, preferred_element_type=jnp.float32)  3.65 us
  transfers between devices with their start and end apart: 3, of which 2 were waited for; matrix products, arithmetic and copies ran while one was open for 17% of the time, Pallas kernels for 0%

commit v1 on v0

v1 whole, which is shorter than its diff:
```python
import jax
import jax.numpy as jnp
from jax import lax
from jax.sharding import PartitionSpec as P

BETA = 0.9
HIGH = lax.Precision.HIGH
F32 = jnp.float32
BF16 = jnp.bfloat16


def dot(left, right, precision=None):
    return jnp.dot(left, right, precision=precision, preferred_element_type=F32)


def add(left, right):
    return (left.astype(F32) + right.astype(F32)).astype(BF16)


def ring_sum(local, dp_size):
    chips = dp_size // 2
    half = chips // 2
    me = lax.axis_index("dp")
    z, core = me // 2, me % 2
    groups = local.shape[0] // dp_size
    grouped = local.reshape(chips, 2, groups, *local.shape[1:])
    sibling = [(i, i ^ 1) for i in range(dp_size)]
    right = [(i, (i + 2) % dp_size) for i in range(dp_size)]
    left = [(i, (i - 2) % dp_size) for i in range(dp_size)]

    def chunk(distance, which):
        start = (lax.rem(z + distance + chips, chips), which) + (0,) * (grouped.ndim - 2)
        return lax.dynamic_slice(grouped, start, (1, 1) + grouped.shape[2:])[0, 0]

    paired = {}
    for distance in range(half, -1, -1):
        offsets = [distance] if distance in (0, half) else [distance, -distance]
        away = jnp.stack([chunk(d, 1 - core) for d in offsets])
        came = lax.ppermute(away, "dp", sibling)
        for k, d in enumerate(offsets):
            paired[d] = add(chunk(d, core), came[k])
    cut = groups // 2
    from_left = lax.ppermute(paired[half][:cut], "dp", right)
    from_right = lax.ppermute(paired[half][cut:], "dp", left)
    for distance in range(half - 1, 0, -1):
        go_right, go_left = paired[distance], paired[-distance]
        if distance == half - 1:
            go_right = jnp.concatenate([add(go_right[:cut], from_left), go_right[cut:]])
            go_left = jnp.concatenate([go_left[:cut], add(go_left[cut:], from_right)])
        else:
            go_right, go_left = add(go_right, from_left), add(go_left, from_right)
        from_left = lax.ppermute(go_right, "dp", right)
        from_right = lax.ppermute(go_left, "dp", left)
    total = paired[0].astype(F32) + from_left.astype(F32) + from_right.astype(F32)
    return total.astype(BF16)


def prepare(factor, root):
    square = dot(root, root)
    fourth = dot(square, square, HIGH)
    return fourth, BETA * dot(fourth, factor, HIGH)


def refresh(fourth, product, gram, root):
    product = product + dot(fourth, gram, HIGH)
    order = product.shape[0]
    identity = jnp.eye(order, dtype=F32)
    e1 = 0.25 * (identity - product)
    e2 = dot(e1, e1, HIGH)
    inner = dot(e2, 4.75 * e1 + e2, HIGH)
    correction = e1 + dot(e2, 2.5 * identity + 7.5 * e1 + 8.75 * e2 + inner, HIGH)
    return root.astype(F32) + dot(root, correction.astype(BF16))


def body(partials, l_factor, r_factor, l_root, r_root, owner_table):
    owners = lax.axis_size("owner")
    dp_size = lax.axis_size("dp")
    group_index = lax.axis_index("dp")
    owner_index = lax.axis_index("owner")
    my_row = lax.dynamic_index_in_dim(owner_table, group_index, 0, keepdims=False)
    slice_rows, row_width = partials.shape[2:]
    row_blocks = my_row.shape[0]
    owner_ids = jnp.arange(owners, dtype=jnp.int32)
    l_old, r_old, l_inv, r_inv = l_factor[0], r_factor[0], l_root[0], r_root[0]
    l_fourth, l_product = prepare(l_old, l_inv)
    r_fourth, r_product = prepare(r_old, r_inv)
    summed = ring_sum(partials[0], dp_size)
    select = owner_ids[:, None] == my_row[None, :]
    outgoing = jnp.sum(
        jnp.where(select[:, :, None, None], summed[None], jnp.zeros((), BF16)), axis=1, dtype=BF16
    )
    arrived = lax.all_to_all(outgoing, "owner", split_axis=0, concat_axis=0, tiled=True)
    gradient = arrived.reshape(owners * slice_rows, row_width)
    is_owner = jnp.any(my_row == owner_index)
    left_applied = dot(l_inv, gradient).astype(BF16)
    precond = dot(left_applied, r_inv).astype(BF16)
    returned = lax.all_to_all(
        precond.reshape(owners, slice_rows, row_width),
        "owner",
        split_axis=0,
        concat_axis=0,
        tiled=True,
    )
    my_blocks = jnp.take(returned, my_row, axis=0, mode="clip")
    l_gram = (1.0 - BETA) * dot(gradient, gradient.T)
    r_gram = (1.0 - BETA) * dot(gradient.T, gradient)
    l_new = BETA * l_old + l_gram
    r_new = BETA * r_old + r_gram
    l_next = refresh(l_fourth, l_product, l_gram, l_inv).astype(BF16)
    r_next = refresh(r_fourth, r_product, r_gram, r_inv).astype(BF16)
    l_out = jnp.where(is_owner, l_new, l_old)[None]
    r_out = jnp.where(is_owner, r_new, r_old)[None]
    l_root_out = jnp.where(is_owner, l_next, l_inv)[None]
    r_root_out = jnp.where(is_owner, r_next, r_inv)[None]
    return (my_blocks, l_out, r_out, l_root_out, r_root_out)


def solution(mesh):
    placed = (
        P("dp", None, "owner", None),
        P(("dp", "owner"), None, None),
        P(("dp", "owner"), None, None),
        P(("dp", "owner"), None, None),
        P(("dp", "owner"), None, None),
        P(),
    )
    return jax.shard_map(
        body,
        mesh=mesh,
        in_specs=placed,
        out_specs=(
            P("dp", "owner", None),
            P(("dp", "owner"), None, None),
            P(("dp", "owner"), None, None),
            P(("dp", "owner"), None, None),
            P(("dp", "owner"), None, None),
        ),
        check_vma=False,
    )
```

time: 152 us -> 102 us (0.67)
  waiting for transfers between devices: 69.2 us -> 23.8 us
  starting transfers between devices: 13.8 us -> 29.5 us
  matrix products: 45.6 us -> 31.4 us
  between operations: 14.3 us -> 1.07 us
  other arithmetic: 3.07 us -> 10 us
    reduce_scatter x1 -> x0, waiting for transfers between devices: 64.7 us -> none  [body(): lax.psum_scatter(local_rows.astype(jnp.float32).astype(jnp.bfloat16), 'dp...]
    ppermute x0 -> x13, waiting for transfers between devices: none -> 19.9 us  [the longest x3 9.09 us: ring_sum(): from_right = lax.ppermute(go_left, 'dp', left)]
    ppermute x0 -> x13, starting transfers between devices: none -> 15.4 us  [the longest x1 5.93 us: ring_sum(): from_right = lax.ppermute(paired[half][cut:], 'dp', left)]
    dot_general x21 -> x19, matrix products: 45.6 us -> 31.4 us  [dot(): return jnp.dot(left, right, precision=precision, preferred_element_type=F32)]
    convert_element_type x0 -> x6, other arithmetic: none -> 5.45 us  [the longest x5 4.24 us: add(): return (left.astype(F32) + right.astype(F32)).astype(BF16)]
    unnamed x36 -> x22, local copies, waits for them, and re-layouts: 5.31 us -> 0.85 us
    another operation x0 -> x1, local copies, waits for them, and re-layouts: none -> 2.4 us  [ring_sum(): away = jnp.stack([chunk(d, 1 - core) for d in offsets])]
    gather x0 -> x1, local copies, waits for them, and re-layouts: none -> 2.31 us  [body(): my_blocks = jnp.take(returned, my_row, axis=0, mode='clip')]
  transfers between devices with their start and end apart: 3 -> 15, of which waited for: 2 -> 10; matrix products, arithmetic and copies ran while one was open for 17% -> 22% of each run, Pallas kernels for 0% -> 0%
where the time goes in v1:
time: 102 us
  matrix products  31.4 us (31%)
  starting transfers between devices  29.5 us (29%)
  waiting for transfers between devices  23.8 us (23%)
  other arithmetic  10 us (10%)
  local copies, waits for them, and re-layouts  5.78 us (6%)
  between operations  1.07 us (1%)
    dot_general x19, matrix products, dot(): return jnp.dot(left, right, precision=precision, preferred_element_type=F32)  31.4 us
    ppermute x3, waiting for transfers between devices, ring_sum(): from_right = lax.ppermute(go_left, 'dp', left)  9.09 us
    all_to_all x1, starting transfers between devices, body(): lax.all_to_all(outgoing, 'owner', split_axis=0, concat_axis=0, tiled=True)  7.46 us
    ppermute x3, waiting for transfers between devices, ring_sum(): from_left = lax.ppermute(go_right, 'dp', right)  7.02 us
    all_to_all x1, starting transfers between devices, body(): lax.all_to_all(precond.reshape(owners, slice_rows, row_width), 'owner', s...  6.6 us
    ppermute x1, starting transfers between devices, ring_sum(): from_right = lax.ppermute(paired[half][cut:], 'dp', left)  5.93 us
    convert_element_type x5, other arithmetic, add(): return (left.astype(F32) + right.astype(F32)).astype(BF16)  4.24 us
    ppermute x3, starting transfers between devices, ring_sum(): from_left = lax.ppermute(go_right, 'dp', right)  4.03 us
  transfers between devices with their start and end apart: 15, of which 10 were waited for; matrix products, arithmetic and copies ran while one was open for 22% of the time, Pallas kernels for 0%

profile of v1, /device:TPU:4, one launch (start us, length us, event | category | flops | bytes accessed | tf_op | source)
XLA Modules:
  0.0 101.6 jit_solution(8255900760174219375)
XLA Ops:
  0.8 2.4 %dynamic-slice_bitcast_fusion.7 = (bf16[1,8,32,512]{3,2,1,0:T(8,128)(2,1)S(1)}, bf16[1,8,32,512]{3,2,1,0:T(8,128)(2,1)}, bf16[1,8,32,512]{3,2,1,0:T(8,128)(2,1)S...) fusion(bf16[8,2,8,32,512]{4,3,2,1,0:T(8,128)(2,1)} %bitcast.173, ...), kind=kLoop, calls=%fused_computation.107 | loop fusion | bytes 4194340 | tf_op jit(solution)/shard_map/stack;squeeze | solution.py:38
  5.2 1.2 %collective-permute-done.4 = bf16[1,8,32,512]{3,2,1,0:T(8,128)(2,1)} collective-permute-done((bf16[1,8,32,512]{3,2,1,0:T(8,128)(2,1)}, bf16[1,8,32,512]{3,2,1,0:T(8,128)(2,1)}, u32[]{:S(2)}, u32[]{:S(2)}) %collective-permute-start.4) | collective-permute-done | bytes 262176 | tf_op jit(solution)/shard_map/ppermute | solution.py:39
  6.3 1.4 %fusion.39 = (bf16[8,32,512]{2,1,0:T(8,128)(2,1)S(1)}, bf16[8,32,512]{2,1,0:T(8,128)(2,1)S(1)}, bf16[8,32,512]{2,1,0:T(8,128)(2,1)S(1)}) fusion(bf16[2,8,32,512]{3,2,1,0:T(8,128)(2,1)S(1)} %collective-permute-done.3, bf16[8,2,8,32,512]{4,3,2,1,0:T(8,128)(2,1)} %bitcast.174, s32[]{:T(128)S(6)} %select_n.103, s32[]{:T(128)S(6)} %select_n.97, ...), kind=kLoop, calls=%fused_computation.66 | loop fusion | flops 1572864 | bytes 2359312 | tf_op jit(solution)/shard_map/convert_element_type | solution.py:17
  7.8 5.9 %collective-permute-start.9 = (bf16[4,32,512]{2,1,0:T(8,128)(2,1)S(1)}, bf16[4,32,512]{2,1,0:T(8,128)(2,1)S(1)}, u32[]{:S(2)}, u32[]{:S(2)}) collective-permute-start(bf16[4,32,512]{2,1,0:T(8,128)(2,1)S(1)} %get-tuple-element.21), channel_id=1, source_target_pairs={{0,224},{16,240},{32,0},{48,16},{64,32},{80,48},{96,64},{112,80},{... | collective-permute-start | bytes 393224 | tf_op jit(solution)/shard_map/ppermute | solution.py:44
  14.9 1.9 %collective-permute-done.9 = bf16[4,32,512]{2,1,0:T(8,128)(2,1)S(1)} collective-permute-done((bf16[4,32,512]{2,1,0:T(8,128)(2,1)S(1)}, bf16[4,32,512]{2,1,0:T(8,128)(2,1)S(1)}, u32[]{:S(2)}, u32[]{:S(2)}) %collective-permute-start.9) | collective-permute-done | bytes 131104 | tf_op jit(solution)/shard_map/ppermute | solution.py:44
  16.9 3.8 %collective-permute-start.10 = (bf16[8,32,512]{2,1,0:T(8,128)(2,1)S(1)}, bf16[8,32,512]{2,1,0:T(8,128)(2,1)S(1)}, u32[]{:S(2)}, u32[]{:S(2)}) collective-permute-start(bf16[8,32,512]{2,1,0:T(8,128)(2,1)S(1)} %pad_maximum_fusion.4), channel_id=1, source_target_pairs={{0,224},{16,240},{32,0},{48,16},{64,32},{80,48},{96,64},{112,80},{... | collective-permute-start | bytes 786440 | tf_op jit(solution)/shard_map/ppermute | solution.py:53
  22.0 3.7 %collective-permute-done.10 = bf16[8,32,512]{2,1,0:T(8,128)(2,1)S(1)} collective-permute-done((bf16[8,32,512]{2,1,0:T(8,128)(2,1)S(1)}, bf16[8,32,512]{2,1,0:T(8,128)(2,1)S(1)}, u32[]{:S(2)}, u32[]{:S(2)}) %collective-permute-start.10) | collective-permute-done | bytes 262176 | tf_op jit(solution)/shard_map/ppermute | solution.py:53
  25.7 4.2 %collective-permute-done.6 = bf16[8,32,512]{2,1,0:T(8,128)(2,1)S(1)} collective-permute-done((bf16[8,32,512]{2,1,0:T(8,128)(2,1)S(1)}, bf16[8,32,512]{2,1,0:T(8,128)(2,1)S(1)}, u32[]{:S(2)}, u32[]{:S(2)}) %collective-permute-start.6) | collective-permute-done | bytes 262176 | tf_op jit(solution)/shard_map/ppermute | solution.py:52
  29.9 1.4 %add_convert_fusion.4 = (bf16[8,32,512]{2,1,0:T(8,128)(2,1)S(1)}, bf16[8,32,512]{2,1,0:T(8,128)(2,1)S(1)}) fusion(bf16[8,32,512]{2,1,0:T(8,128)(2,1)S(1)} %collective-permute-done.6, bf16[2,8,32,512]{3,2,1,0:T(8,128)(2,1)} %collective-permute-done.2, bf16[8,2,8,32,512]{4,3,2,1,0:T(8,128)(2,1)} %bitcast.175, s32[]{:T(128)S(6)} %select_n.101, ...), kind=kLoop, calls=%fused_computation.89 | loop fusion | flops 2097152 | bytes 2097164 | tf_op jit(solution)/shard_map/convert_element_type | solution.py:17
  31.5 2.0 %collective-permute-start.7 = (bf16[8,32,512]{2,1,0:T(8,128)(2,1)S(1)}, bf16[8,32,512]{2,1,0:T(8,128)(2,1)S(1)}, u32[]{:S(2)}, u32[]{:S(2)}) collective-permute-start(bf16[8,32,512]{2,1,0:T(8,128)(2,1)S(1)} %get-tuple-element.7), channel_id=1, source_target_pairs={{0,32},{16,48},{32,64},{48,80},{64,96},{80,112},{96,128},{112,144}... | collective-permute-start | bytes 786440 | tf_op jit(solution)/shard_map/ppermute | solution.py:52
  34.5 3.3 %collective-permute-done.11 = bf16[8,32,512]{2,1,0:T(8,128)(2,1)S(1)} collective-permute-done((bf16[8,32,512]{2,1,0:T(8,128)(2,1)S(1)}, bf16[8,32,512]{2,1,0:T(8,128)(2,1)S(1)}, u32[]{:S(2)}, u32[]{:S(2)}) %collective-permute-start.11) | collective-permute-done | bytes 262176 | tf_op jit(solution)/shard_map/ppermute | solution.py:53
  37.8 1.3 %collective-permute-done.7 = bf16[8,32,512]{2,1,0:T(8,128)(2,1)S(1)} collective-permute-done((bf16[8,32,512]{2,1,0:T(8,128)(2,1)S(1)}, bf16[8,32,512]{2,1,0:T(8,128)(2,1)S(1)}, u32[]{:S(2)}, u32[]{:S(2)}) %collective-permute-start.7) | collective-permute-done | bytes 262176 | tf_op jit(solution)/shard_map/ppermute | solution.py:52
  39.1 1.3 %add_convert_fusion.3 = (bf16[8,32,512]{2,1,0:T(8,128)(2,1)S(1)}, bf16[8,32,512]{2,1,0:T(8,128)(2,1)S(1)}) fusion(bf16[8,32,512]{2,1,0:T(8,128)(2,1)S(1)} %collective-permute-done.7, bf16[2,8,32,512]{3,2,1,0:T(8,128)(2,1)S(1)} %collective-permute-done.1, bf16[8,2,8,32,512]{4,3,2,1,0:T(8,128)(2,1)} %bitcast.176, s32[]{:T(128)S(6)} %select_n.99, ...), kind=kLoop, calls=%fused_computation.88 | loop fusion | flops 2097152 | bytes 2097164 | tf_op jit(solution)/shard_map/convert_element_type | solution.py:17
  40.6 1.9 %collective-permute-start.8 = (bf16[8,32,512]{2,1,0:T(8,128)(2,1)S(1)}, bf16[8,32,512]{2,1,0:T(8,128)(2,1)S(1)}, u32[]{:S(2)}, u32[]{:S(2)}) collective-permute-start(bf16[8,32,512]{2,1,0:T(8,128)(2,1)S(1)} %get-tuple-element.5), channel_id=1, source_target_pairs={{0,32},{16,48},{32,64},{48,80},{64,96},{80,112},{96,128},{112,144}... | collective-permute-start | bytes 786440 | tf_op jit(solution)/shard_map/ppermute | solution.py:52
  42.5 2.0 %convolution_multiply_fusion = f32[512,512]{1,0:T(8,128)} fusion(f32[512,512]{1,0:T(8,128)S(1)} %fusion.63, f32[1,512,512]{2,1,0:T(8,128)S(1)} %copy-done.2), kind=kOutput, calls=%fused_computation.18 | convolution fusion | flops 805568512 | bytes 3145728 | tf_op jit(solution)/shard_map/dot_general | solution.py:13
  44.7 2.1 %collective-permute-done.12 = bf16[8,32,512]{2,1,0:T(8,128)(2,1)S(1)} collective-permute-done((bf16[8,32,512]{2,1,0:T(8,128)(2,1)S(1)}, bf16[8,32,512]{2,1,0:T(8,128)(2,1)S(1)}, u32[]{:S(2)}, u32[]{:S(2)}) %collective-permute-start.12) | collective-permute-done | bytes 262176 | tf_op jit(solution)/shard_map/ppermute | solution.py:53
  46.9 1.5 %collective-permute-done.8 = bf16[8,32,512]{2,1,0:T(8,128)(2,1)S(1)} collective-permute-done((bf16[8,32,512]{2,1,0:T(8,128)(2,1)S(1)}, bf16[8,32,512]{2,1,0:T(8,128)(2,1)S(1)}, u32[]{:S(2)}, u32[]{:S(2)}) %collective-permute-start.8) | collective-permute-done | bytes 262176 | tf_op jit(solution)/shard_map/ppermute | solution.py:52
  48.3 1.2 %add_convert_fusion = bf16[8,32,512]{2,1,0:T(8,128)(2,1)S(1)} fusion(bf16[8,32,512]{2,1,0:T(8,128)(2,1)S(1)} %collective-permute-done.12, bf16[8,32,512]{2,1,0:T(8,128)(2,1)S(1)} %collective-permute-done.8, bf16[1,8,32,512]{3,2,1,0:T(8,128)(2,1)} %collective-permute-done, bf16[8,2,8,32,512]{4,3,2,1,0:T(8,128)(2,1)} %bitcast.177, s32[]{:T(128)S(6)} %select_n.95, ...), kind=kLoop, calls=%fused_computation.85 | loop fusion | flops 1310720 | bytes 1310728 | tf_op jit(solution)/shard_map/convert_element_type | solution.py:55
  49.5 1.3 %select_reduce_fusion = bf16[16,32,512]{2,1,0:T(8,128)(2,1)} fusion(pred[16,8]{1,0:T(8,128)(4,1)S(1)} %iota_compare_fusion.1, bf16[8,32,512]{2,1,0:T(8,128)(2,1)S(1)} %add_convert_fusion), kind=kLoop, calls=%fused_computation.1 | loop fusion | flops 3932160 | bytes 786560 | tf_op jit(solution)/shard_map/reduce_sum | solution.py:89
  50.8 7.5 %all-to-all-start = ((bf16[16,32,512]{2,1,0:T(8,128)(2,1)}), bf16[16,32,512]{2,1,0:T(8,128)(2,1)S(1)}, u32[]{:S(2)}, u32[]{:S(2)}) async-start(bf16[16,32,512]{2,1,0:T(8,128)(2,1)} %select_reduce_fusion), calls=%async_computation | async-start | bytes 1048576 | tf_op jit(solution)/shard_map/all_to_all | solution.py:92
  58.9 3.2 %convolution_multiply_fusion.1 = f32[512,512]{1,0:T(8,128)} fusion(f32[512,512]{1,0:T(8,128)S(1)} %fusion.62, f32[1,512,512]{2,1,0:T(8,128)} %param.7), kind=kOutput, calls=%fused_computation.21 | convolution fusion | flops 805568512 | bytes 3145728 | tf_op jit(solution)/shard_map/dot_general | solution.py:13
  62.1 3.9 %all-to-all-done = bf16[16,32,512]{2,1,0:T(8,128)(2,1)S(1)} async-done(((bf16[16,32,512]{2,1,0:T(8,128)(2,1)}), bf16[16,32,512]{2,1,0:T(8,128)(2,1)S(1)}, u32[]{:S(2)}, u32[]{:S(2)}) %all-to-all-start) | async-done | bytes 524320 | tf_op jit(solution)/shard_map/all_to_all | solution.py:92
  66.8 1.9 %convolution_multiply_fusion.2 = f32[512,512]{1,0:T(8,128)S(1)} fusion(bf16[512,512]{1,0:T(8,128)(2,1)} %bitcast.171), kind=kOutput, calls=%fused_computation.24 | convolution fusion | flops 268697600 | bytes 1572864 | tf_op jit(solution)/shard_map/dot_general | solution.py:13
  68.7 3.0 %convolution_convert_fusion = bf16[512,512]{1,0:T(8,128)(2,1)} fusion(bf16[512,512]{1,0:T(8,128)(2,1)} %bitcast.172, bf16[1,512,512]{2,1,0:T(8,128)(2,1)} %param.10, bf16[1,512,512]{2,1,0:T(8,128)(2,1)} %param.9), kind=kOutput, calls=%fused_computation.27 | convolution fusion | flops 537395200 | bytes 2097152 | tf_op jit(solution)/shard_map/dot_general | solution.py:13
  71.7 1.8 %fusion.12 = f32[512,512]{1,0:T(8,128)S(1)} fusion(bf16[16,32,512]{2,1,0:T(8,128)(2,1)} %copy-done.1), kind=kOutput, calls=%fused_computation.23 | convolution fusion | flops 268697600 | bytes 1572864 | tf_op jit(solution)/shard_map/dot_general | solution.py:13
  76.8 1.8 %fusion.14 = bf16[512,512]{1,0:T(8,128)(2,1)} fusion(f32[512,512]{1,0:T(8,128)S(1)} %fusion.31, f32[512,512]{1,0:T(8,128)S(1)} %fusion.7, f32[512,512]{1,0:T(8,128)S(1)} %convert_subtract_fusion), kind=kOutput, calls=%fused_computation.26 | convolution fusion | flops 806092800 | bytes 3670016 | tf_op jit(solution)/shard_map/dot_general | solution.py:13
  81.8 1.8 %fusion.13 = bf16[512,512]{1,0:T(8,128)(2,1)} fusion(f32[512,512]{1,0:T(8,128)S(1)} %fusion.33, f32[512,512]{1,0:T(8,128)S(1)} %fusion.4, f32[512,512]{1,0:T(8,128)S(1)} %convert_subtract_fusion.1), kind=kOutput, calls=%fused_computation.25 | convolution fusion | flops 806092800 | bytes 3670016 | tf_op jit(solution)/shard_map/dot_general | solution.py:13
  83.6 6.6 %all-to-all-start.1 = ((bf16[16,32,512]{2,1,0:T(8,128)(2,1)}), bf16[16,32,512]{2,1,0:T(8,128)(2,1)}, u32[]{:S(2)}, u32[]{:S(2)}) async-start(bf16[16,32,512]{2,1,0:T(8,128)(2,1)} %bitcast.178), calls=%async_computation.1 | async-start | bytes 1048576 | tf_op jit(solution)/shard_map/all_to_all | solution.py:97
  90.3 3.3 %fusion.19 = bf16[1,512,512]{2,1,0:T(8,128)(2,1)} fusion(bf16[512,512]{1,0:T(8,128)(2,1)} %fusion.14, bf16[1,512,512]{2,1,0:T(8,128)(2,1)} %param.10, pred[]{:T(512)} %compare_reduce_fusion), kind=kOutput, calls=%fused_computation.33 | convolution fusion | flops 269484032 | bytes 1572865 | tf_op jit(solution)/shard_map/dot_general | solution.py:13
  93.6 3.2 %fusion.20 = bf16[1,512,512]{2,1,0:T(8,128)(2,1)} fusion(bf16[512,512]{1,0:T(8,128)(2,1)} %fusion.13, bf16[1,512,512]{2,1,0:T(8,128)(2,1)} %param.9, pred[]{:T(512)} %compare_reduce_fusion), kind=kOutput, calls=%fused_computation.34 | convolution fusion | flops 269484032 | bytes 1572865 | tf_op jit(solution)/shard_map/dot_general | solution.py:13
  96.8 2.5 %fusion.25 = (f32[1,512,512]{2,1,0:T(8,128)}, f32[1,512,512]{2,1,0:T(8,128)}) fusion(f32[512,512]{1,0:T(8,128)S(1)} %copy-done.7, f32[1,512,512]{2,1,0:T(8,128)S(1)} %copy-done.3, pred[]{:T(512)} %compare_reduce_fusion, f32[512,512]{1,0:T(8,128)S(1)} %convolution_multiply_fusion.2, f32[1,512,512]{2,1,0:T(8,128)S(1)} %copy-done.4), kind=kLoop, calls=%fused_computation.41 | loop fusion | flops 1572864 | bytes 6291457 | tf_op jit(solution)/shard_map/broadcast_in_dim | solution.py:112
  99.3 2.3 %gather_fusion = bf16[8,32,512]{2,1,0:T(8,128)(2,1)} fusion(bf16[16,32,512]{2,1,0:T(8,128)(2,1)} %all-to-all-done.1, s32[1024]{0:T(1024)S(1)} %pad_clamp_fusion), kind=kCustom, calls=%fused_computation | custom fusion | bytes 524320 | tf_op jit(solution)/shard_map/jit(_take)/gather | solution.py:104
  (61 shorter events, 13.8 us)
Async XLA Ops:
  0.6 43.9 %copy-start = (s32[16,8]{0,1:T(8,128)S(1)}, s32[16,8]{0,1:T(8,128)}, u32[]{:S(2)}) copy-start(s32[16,8]{0,1:T(8,128)} %param.11) | copy-start | bytes 1540
  0.6 4.1 %copy-start.9 = (bf16[1,512,512]{2,1,0:T(8,128)(2,1)S(1)}, bf16[1,512,512]{2,1,0:T(8,128)(2,1)}, u32[]{:S(2)}) copy-start(bf16[1,512,512]{2,1,0:T(8,128)(2,1)} %param.10) | copy-start | bytes 1572868
  3.2 3.1 %collective-permute-start.3 = (bf16[2,8,32,512]{3,2,1,0:T(8,128)(2,1)S(1)}, bf16[2,8,32,512]{3,2,1,0:T(8,128)(2,1)S(1)}, u32[]{:S(2)}, u32[]{:S(2)}) collective-permute-start(bf16[2,8,32,512]{3,2,1,0:T(8,128)(2,1)S(1)} %pad_maximum_fusion.2), channel_id=1, source_target_pairs={{0,16},{16,0},{32,48},{48,32},{64,80},{80,64},{96,112},{112,96},{1... | collective-permute-start | bytes 1572872 | tf_op jit(solution)/shard_map/ppermute | solution.py:39
  3.3 3.0 %collective-permute-start.4 = (bf16[1,8,32,512]{3,2,1,0:T(8,128)(2,1)}, bf16[1,8,32,512]{3,2,1,0:T(8,128)(2,1)}, u32[]{:S(2)}, u32[]{:S(2)}) collective-permute-start(bf16[1,8,32,512]{3,2,1,0:T(8,128)(2,1)} %get-tuple-element.12), channel_id=1, source_target_pairs={{0,16},{16,0},{32,48},{48,32},{64,80},{80,64},{96,112},{112,96},{1... | collective-permute-start | bytes 786440 | tf_op jit(solution)/shard_map/ppermute | solution.py:39
  3.9 18.1 %collective-permute-start.2 = (bf16[2,8,32,512]{3,2,1,0:T(8,128)(2,1)S(1)}, bf16[2,8,32,512]{3,2,1,0:T(8,128)(2,1)}, u32[]{:S(2)}, u32[]{:S(2)}) collective-permute-start(bf16[2,8,32,512]{3,2,1,0:T(8,128)(2,1)S(1)} %pad_maximum_fusion.1), channel_id=1, source_target_pairs={{0,16},{16,0},{32,48},{48,32},{64,80},{80,64},{96,112},{112,96},{1... | collective-permute-start | bytes 1572872 | tf_op jit(solution)/shard_map/ppermute | solution.py:39
  4.1 30.4 %collective-permute-start.1 = (bf16[2,8,32,512]{3,2,1,0:T(8,128)(2,1)S(1)}, bf16[2,8,32,512]{3,2,1,0:T(8,128)(2,1)S(1)}, u32[]{:S(2)}, u32[]{:S(2)}) collective-permute-start(bf16[2,8,32,512]{3,2,1,0:T(8,128)(2,1)S(1)} %pad_maximum_fusion), channel_id=1, source_target_pairs={{0,16},{16,0},{32,48},{48,32},{64,80},{80,64},{96,112},{112,96},{1... | collective-permute-start | bytes 1572872 | tf_op jit(solution)/shard_map/ppermute | solution.py:39
  4.6 40.1 %collective-permute-start = (bf16[1,8,32,512]{3,2,1,0:T(8,128)(2,1)S(1)}, bf16[1,8,32,512]{3,2,1,0:T(8,128)(2,1)}, u32[]{:S(2)}, u32[]{:S(2)}) collective-permute-start(bf16[1,8,32,512]{3,2,1,0:T(8,128)(2,1)S(1)} %get-tuple-element.11), channel_id=1, source_target_pairs={{0,16},{16,0},{32,48},{48,32},{64,80},{80,64},{96,112},{112,96},{1... | collective-permute-start | bytes 786440 | tf_op jit(solution)/shard_map/ppermute | solution.py:39
  5.2 16.4 %copy-start.10 = (bf16[1,512,512]{2,1,0:T(8,128)(2,1)S(1)}, bf16[1,512,512]{2,1,0:T(8,128)(2,1)}, u32[]{:S(2)}) copy-start(bf16[1,512,512]{2,1,0:T(8,128)(2,1)} %param.9) | copy-start | bytes 1572868
  7.8 9.0 %collective-permute-start.9 = (bf16[4,32,512]{2,1,0:T(8,128)(2,1)S(1)}, bf16[4,32,512]{2,1,0:T(8,128)(2,1)S(1)}, u32[]{:S(2)}, u32[]{:S(2)}) collective-permute-start(bf16[4,32,512]{2,1,0:T(8,128)(2,1)S(1)} %get-tuple-element.21), channel_id=1, source_target_pairs={{0,224},{16,240},{32,0},{48,16},{64,32},{80,48},{96,64},{112,80},{... | collective-permute-start | bytes 393224 | tf_op jit(solution)/shard_map/ppermute | solution.py:44
  14.8 6.5 %collective-permute-start.5 = (bf16[4,32,512]{2,1,0:T(8,128)(2,1)S(1)}, bf16[4,32,512]{2,1,0:T(8,128)(2,1)S(1)}, u32[]{:S(2)}, u32[]{:S(2)}) collective-permute-start(bf16[4,32,512]{2,1,0:T(8,128)(2,1)S(1)} %get-tuple-element.20), channel_id=1, source_target_pairs={{0,32},{16,48},{32,64},{48,80},{64,96},{80,112},{96,128},{112,144}... | collective-permute-start | bytes 393224 | tf_op jit(solution)/shard_map/ppermute | solution.py:43
  16.9 8.8 %collective-permute-start.10 = (bf16[8,32,512]{2,1,0:T(8,128)(2,1)S(1)}, bf16[8,32,512]{2,1,0:T(8,128)(2,1)S(1)}, u32[]{:S(2)}, u32[]{:S(2)}) collective-permute-start(bf16[8,32,512]{2,1,0:T(8,128)(2,1)S(1)} %pad_maximum_fusion.4), channel_id=1, source_target_pairs={{0,224},{16,240},{32,0},{48,16},{64,32},{80,48},{96,64},{112,80},{... | collective-permute-start | bytes 786440 | tf_op jit(solution)/shard_map/ppermute | solution.py:53
  21.4 21.1 %copy-start.2 = (f32[1,512,512]{2,1,0:T(8,128)S(1)}, f32[1,512,512]{2,1,0:T(8,128)}, u32[]{:S(2)}) copy-start(f32[1,512,512]{2,1,0:T(8,128)} %param.8) | copy-start | bytes 3145732
  21.4 8.5 %collective-permute-start.6 = (bf16[8,32,512]{2,1,0:T(8,128)(2,1)S(1)}, bf16[8,32,512]{2,1,0:T(8,128)(2,1)S(1)}, u32[]{:S(2)}, u32[]{:S(2)}) collective-permute-start(bf16[8,32,512]{2,1,0:T(8,128)(2,1)S(1)} %pad_maximum_fusion.3), channel_id=1, source_target_pairs={{0,32},{16,48},{32,64},{48,80},{64,96},{80,112},{96,128},{112,144}... | collective-permute-start | bytes 786440 | tf_op jit(solution)/shard_map/ppermute | solution.py:52
  31.4 6.5 %collective-permute-start.11 = (bf16[8,32,512]{2,1,0:T(8,128)(2,1)S(1)}, bf16[8,32,512]{2,1,0:T(8,128)(2,1)S(1)}, u32[]{:S(2)}, u32[]{:S(2)}) collective-permute-start(bf16[8,32,512]{2,1,0:T(8,128)(2,1)S(1)} %get-tuple-element.8), channel_id=1, source_target_pairs={{0,224},{16,240},{32,0},{48,16},{64,32},{80,48},{96,64},{112,80},{... | collective-permute-start | bytes 786440 | tf_op jit(solution)/shard_map/ppermute | solution.py:53
  31.5 7.7 %collective-permute-start.7 = (bf16[8,32,512]{2,1,0:T(8,128)(2,1)S(1)}, bf16[8,32,512]{2,1,0:T(8,128)(2,1)S(1)}, u32[]{:S(2)}, u32[]{:S(2)}) collective-permute-start(bf16[8,32,512]{2,1,0:T(8,128)(2,1)S(1)} %get-tuple-element.7), channel_id=1, source_target_pairs={{0,32},{16,48},{32,64},{48,80},{64,96},{80,112},{96,128},{112,144}... | collective-permute-start | bytes 786440 | tf_op jit(solution)/shard_map/ppermute | solution.py:52
  40.4 6.5 %collective-permute-start.12 = (bf16[8,32,512]{2,1,0:T(8,128)(2,1)S(1)}, bf16[8,32,512]{2,1,0:T(8,128)(2,1)S(1)}, u32[]{:S(2)}, u32[]{:S(2)}) collective-permute-start(bf16[8,32,512]{2,1,0:T(8,128)(2,1)S(1)} %get-tuple-element.6), channel_id=1, source_target_pairs={{0,224},{16,240},{32,0},{48,16},{64,32},{80,48},{96,64},{112,80},{... | collective-permute-start | bytes 786440 | tf_op jit(solution)/shard_map/ppermute | solution.py:53
  40.6 7.8 %collective-permute-start.8 = (bf16[8,32,512]{2,1,0:T(8,128)(2,1)S(1)}, bf16[8,32,512]{2,1,0:T(8,128)(2,1)S(1)}, u32[]{:S(2)}, u32[]{:S(2)}) collective-permute-start(bf16[8,32,512]{2,1,0:T(8,128)(2,1)S(1)} %get-tuple-element.5), channel_id=1, source_target_pairs={{0,32},{16,48},{32,64},{48,80},{64,96},{80,112},{96,128},{112,144}... | collective-permute-start | bytes 786440 | tf_op jit(solution)/shard_map/ppermute | solution.py:52
  50.8 15.2 %all-to-all-start = ((bf16[16,32,512]{2,1,0:T(8,128)(2,1)}), bf16[16,32,512]{2,1,0:T(8,128)(2,1)S(1)}, u32[]{:S(2)}, u32[]{:S(2)}) async-start(bf16[16,32,512]{2,1,0:T(8,128)(2,1)} %select_reduce_fusion), calls=%async_computation | async-start | bytes 1048576 | tf_op jit(solution)/shard_map/all_to_all | solution.py:92
  66.0 0.8 copy-start.1
  71.7 1.9 %copy-start.5 = (f32[512,512]{1,0:T(8,128)S(1)}, f32[512,512]{1,0:T(8,128)}, u32[]{:S(2)}) copy-start(f32[512,512]{1,0:T(8,128)} %convolution_multiply_fusion) | copy-start | bytes 3145732
  73.5 1.1 %copy-start.6 = (f32[512,512]{1,0:T(8,128)}, f32[512,512]{1,0:T(8,128)S(1)}, u32[]{:S(2)}) copy-start(f32[512,512]{1,0:T(8,128)S(1)} %fusion.12) | copy-start | bytes 3145732
  75.7 2.9 %copy-start.8 = (f32[512,512]{1,0:T(8,128)S(1)}, f32[512,512]{1,0:T(8,128)}, u32[]{:S(2)}) copy-start(f32[512,512]{1,0:T(8,128)} %convolution_multiply_fusion.1) | copy-start | bytes 3145732
  81.8 15.0 %copy-start.3 = (f32[1,512,512]{2,1,0:T(8,128)S(1)}, f32[1,512,512]{2,1,0:T(8,128)}, u32[]{:S(2)}) copy-start(f32[1,512,512]{2,1,0:T(8,128)} %param.8) | copy-start | bytes 3145732
  83.6 13.2 %copy-start.4 = (f32[1,512,512]{2,1,0:T(8,128)S(1)}, f32[1,512,512]{2,1,0:T(8,128)}, u32[]{:S(2)}) copy-start(f32[1,512,512]{2,1,0:T(8,128)} %param.7) | copy-start | bytes 3145732
  83.6 15.7 %all-to-all-start.1 = ((bf16[16,32,512]{2,1,0:T(8,128)(2,1)}), bf16[16,32,512]{2,1,0:T(8,128)(2,1)}, u32[]{:S(2)}, u32[]{:S(2)}) async-start(bf16[16,32,512]{2,1,0:T(8,128)(2,1)} %bitcast.178), calls=%async_computation.1 | async-start | bytes 1048576 | tf_op jit(solution)/shard_map/all_to_all | solution.py:97
  90.2 6.6 %copy-start.7 = (f32[512,512]{1,0:T(8,128)S(1)}, f32[512,512]{1,0:T(8,128)}, u32[]{:S(2)}) copy-start(f32[512,512]{1,0:T(8,128)} %copy-done.6) | copy-start | bytes 3145732
